TPU v7x, 32 devices: a whole 2x2x4 slice. The times are simulated.
32 devices in a mesh: parts: 2 (over y), region: 4 (over z), feat: 4 (over x, core).
Axes of the slice: x: 2, y: 2, z: 4, core: 2. Of those that a mesh axis runs over, the one named last changes fastest.
Arguments:
- grid_latent: bfloat16 [16384, 512], P(('parts', 'region')), parts along dimension 0, may hold values from -6 to 6
- mesh_latent: bfloat16 [4096, 512], P(('parts', 'region')), parts along dimension 0, may hold values from -6 to 6
- send_tiles: int32 [8, 4, 4], P(('parts', 'region')), parts along dimension 0, may hold values from -1 to 15, as said below
- g2m_sender: int32 [131072], P(('parts', 'region')), parts along dimension 0, may hold values from 0 to 2047, as said below
- g2m_receiver: int32 [131072], P(('parts', 'region')), parts along dimension 0, may hold values from -1 to 511, as said below
- g2m_feature: float32 [4, 131072], P(None, ('parts', 'region')), parts along dimension 1, may hold values from -6 to 6
- m2m_table: int32 [8, 4, 128], P(('parts', 'region')), parts along dimension 0, may hold values from -1 to 511, as said below
- m2m_sender: int32 [65536], P(('parts', 'region')), parts along dimension 0, may hold values from 0 to 511, as said below
- m2m_receiver: int32 [65536], P(('parts', 'region')), parts along dimension 0, may hold values from -1 to 511, as said below
- m2m_feature: float32 [4, 65536], P(None, ('parts', 'region')), parts along dimension 1, may hold values from -6 to 6
- w_send: bfloat16 [2, 512, 512], P(None, None, 'feat'), may hold values from -0.25 to 0.25
- w_recv: bfloat16 [2, 512, 512], P(None, None, 'feat'), may hold values from -0.25 to 0.25
- w_edge_feat: float32 [2, 4, 512], P(None, None, 'feat'), may hold values from -3 to 3
- b_edge: float32 [2, 512], P(None, 'feat'), may hold values from -6 to 6
- w_edge_out: bfloat16 [2, 512, 512], P(None, 'feat'), may hold values from -0.0625 to 0.0625
- b_edge_out: float32 [2, 512], replicated, may hold values from -3 to 3
- w_self: bfloat16 [2, 512, 512], P(None, None, 'feat'), may hold values from -0.25 to 0.25
- w_agg: bfloat16 [2, 512, 512], P(None, None, 'feat'), may hold values from -0.25 to 0.25
- b_node: float32 [2, 512], P(None, 'feat'), may hold values from -6 to 6
- w_node_out: bfloat16 [2, 512, 512], P(None, 'feat'), may hold values from -0.25 to 0.25
- b_node_out: float32 [2, 512], replicated, may hold values from -6 to 6
- norm_gain: float32 [2, 512], replicated, may hold values from 0.1 to 1.9
- norm_shift: float32 [2, 512], replicated, may hold values from -6 to 6
Outputs:
- mesh_encoded: bfloat16 [4096, 512], P(('parts', 'region'), 'feat'), parts along dimension 0
- mesh_processed: bfloat16 [4096, 512], P(('parts', 'region'), 'feat'), parts along dimension 0
There are 2 independent parts, one for each index of `parts`. A program takes and returns all parts, laid end to end along the dimension named above; an argument that names none is the same for every part. Nothing has to cross between parts.
Inputs may be any that keep to these rules, and one draw needn't show every extreme that they name: `send_tiles`: entry [s, d, j] is a tile of region s (rows t * 128 to t * 128 + 127 of it) whose rows region d needs, or -1 for an empty slot; tiles of one [s, d] are distinct and used slots come first; every region uses all 4 slots for itself, and one region uses all 4 slots from every region. `g2m_sender`: an edge of region d names row r of slot j from region s with send_tiles[s, d, j] never -1. `g2m_receiver`: -1 marks an unused edge slot; one region has none. `m2m_table`: entry [d, s, j] is a local mesh node of region s whose sender term region d needs, or -1; distinct within one [d, s], used slots first; every region uses all 128 slots for itself, and one region uses all 128 slots from every region. `m2m_sender`: an edge of region d names slot j from region s with m2m_table[d, s, j] never -1. `m2m_receiver`: -1 marks an unused edge slot; one region has none.
All inputs are finite; a program needn't handle non-finite values.
Results may differ from a plain program's by a relative error of at most 0.018.
Values may be sent and summed in bfloat16 or wider, within the bound.
A program may use at most 64 MiB of HBM per device.

v0:
```python
import jax
import jax.numpy as jnp
from jax import lax
from jax.sharding import PartitionSpec as P

TILE = 128


def swish_unit(value):
    return value * jax.nn.sigmoid(value)


def layer_norm(value, gain, shift):
    center = value - jnp.mean(value, axis=-1, keepdims=True)
    spread = jnp.mean(center * center, axis=-1, keepdims=True)
    return center * lax.rsqrt(spread + 1e-05) * gain + shift


def select_rows(indices, table):
    picks = (indices[:, None] == jnp.arange(table.shape[0], dtype=jnp.int32)[None, :]).astype(
        jnp.bfloat16
    )
    return jnp.dot(picks, table, preferred_element_type=jnp.float32).astype(jnp.bfloat16)


def edge_sums(lookup, senders, receivers, features, recv_proj, w_feat, bias):
    node_count = recv_proj.shape[0]
    edge_count = senders.shape[0]
    edge_block = min(2048, edge_count)
    hidden_width = lookup.shape[1]
    node_ids = jnp.arange(node_count, dtype=jnp.int32)[:, None]
    recv_high = recv_proj.astype(jnp.bfloat16)
    recv_low = (recv_proj - recv_high.astype(jnp.float32)).astype(jnp.bfloat16)
    recv_pair = jnp.concatenate([recv_high, recv_low], axis=1)

    def visit_block(state_pair, start):
        totals, counts = state_pair
        send_part = lax.dynamic_slice_in_dim(senders, start, edge_block)
        recv_part = lax.dynamic_slice_in_dim(receivers, start, edge_block)
        feat_part = lax.dynamic_slice_in_dim(features, start, edge_block, 1)
        member = (node_ids == recv_part[None, :]).astype(jnp.bfloat16)
        picked = lax.dot_general(
            member, recv_pair, (((0,), (0,)), ((), ())), preferred_element_type=jnp.float32
        )
        recv_rows = picked[:, :hidden_width] + picked[:, hidden_width:]
        summed = lookup[send_part].astype(jnp.float32) + recv_rows
        summed = (
            summed
            + jnp.einsum("ke,kh->eh", feat_part, w_feat, precision=lax.Precision.HIGHEST)
            + bias
        )
        hidden = swish_unit(summed).astype(jnp.bfloat16)
        totals = totals + jnp.dot(member, hidden, preferred_element_type=jnp.float32)
        counts = counts + jnp.sum(member.astype(jnp.float32), axis=1)
        return ((totals, counts), None)

    starts = jnp.arange(edge_count // edge_block, dtype=jnp.int32) * edge_block
    initial = (
        jnp.zeros((node_count, hidden_width), jnp.float32),
        jnp.zeros((node_count,), jnp.float32),
    )
    result, unused = lax.scan(visit_block, initial, starts)
    return result


def node_step(
    latent,
    totals,
    counts,
    layer,
    full_outs,
    w_edge_out,
    b_edge_out,
    w_self,
    w_agg,
    b_node,
    w_node_out,
    b_node_out,
    norm_gain,
    norm_shift,
):
    summed = totals.astype(jnp.bfloat16)
    partial_agg = jnp.dot(summed, w_edge_out[layer], preferred_element_type=jnp.float32)
    gathered = (
        lax.psum(partial_agg.astype(jnp.bfloat16), "feat").astype(jnp.float32)
        + counts[:, None] * b_edge_out[layer]
    )
    preact = jnp.dot(latent, w_self[layer], preferred_element_type=jnp.float32)
    preact = (
        preact
        + jnp.dot(gathered.astype(jnp.bfloat16), w_agg[layer], preferred_element_type=jnp.float32)
        + b_node[layer]
    )
    hidden = swish_unit(preact).astype(jnp.bfloat16)
    partial_update = jnp.dot(hidden, w_node_out[layer], preferred_element_type=jnp.float32)
    update = (
        lax.psum(partial_update.astype(jnp.bfloat16), "feat").astype(jnp.float32)
        + b_node_out[layer]
    )
    return (
        latent.astype(jnp.float32) + layer_norm(update, norm_gain[layer], norm_shift[layer])
    ).astype(jnp.bfloat16)


def per_device(
    grid_latent,
    mesh_latent,
    send_tiles,
    g2m_sender,
    g2m_receiver,
    g2m_feature,
    m2m_table,
    m2m_sender,
    m2m_receiver,
    m2m_feature,
    w_send,
    w_recv,
    w_edge_feat,
    b_edge,
    w_edge_out,
    b_edge_out,
    w_self,
    w_agg,
    b_node,
    w_node_out,
    b_node_out,
    norm_gain,
    norm_shift,
):
    full_outs = (w_edge_out, w_node_out)
    node_weights = (
        full_outs,
        w_edge_out,
        b_edge_out,
        w_self,
        w_agg,
        b_node,
        w_node_out,
        b_node_out,
        norm_gain,
        norm_shift,
    )
    regions = lax.axis_size("region")
    hidden_width = w_send.shape[2]
    grid_proj = jnp.dot(grid_latent, w_send[0], preferred_element_type=jnp.float32).astype(
        jnp.bfloat16
    )
    wanted = send_tiles[0]
    tile_table = grid_proj.reshape(-1, TILE * hidden_width)
    tiles = select_rows(wanted.reshape(-1), tile_table).reshape(regions, -1, TILE * hidden_width)
    arrived = lax.all_to_all(tiles, "region", split_axis=0, concat_axis=0, tiled=True)
    grid_lookup = arrived.reshape(-1, hidden_width)
    recv_first = jnp.dot(mesh_latent, w_recv[0], preferred_element_type=jnp.float32)
    totals, counts = edge_sums(
        grid_lookup, g2m_sender, g2m_receiver, g2m_feature, recv_first, w_edge_feat[0], b_edge[0]
    )
    encoded = node_step(mesh_latent, totals, counts, 0, *node_weights)
    mesh_send = jnp.dot(encoded, w_send[1], preferred_element_type=jnp.float32).astype(jnp.bfloat16)
    everything = lax.all_gather(mesh_send, "region", axis=0, tiled=True)
    wanted = m2m_table[0]
    capacity = wanted.shape[1]
    source = m2m_sender // capacity
    row_index = wanted[source, m2m_sender % capacity]
    mesh_index = source * mesh_latent.shape[0] + jnp.maximum(row_index, 0)
    recv_second = jnp.dot(encoded, w_recv[1], preferred_element_type=jnp.float32)
    totals, counts = edge_sums(
        everything, mesh_index, m2m_receiver, m2m_feature, recv_second, w_edge_feat[1], b_edge[1]
    )
    processed = node_step(encoded, totals, counts, 1, *node_weights)
    columns = mesh_latent.shape[1] // lax.axis_size("feat")
    first_column = lax.axis_index("feat") * columns
    return (
        lax.dynamic_slice_in_dim(encoded, first_column, columns, 1),
        lax.dynamic_slice_in_dim(processed, first_column, columns, 1),
    )


def solution(mesh):
    return jax.shard_map(
        per_device,
        mesh=mesh,
        in_specs=(
            P(("parts", "region"), None),
            P(("parts", "region"), None),
            P(("parts", "region"), None, None),
            P(("parts", "region")),
            P(("parts", "region")),
            P(None, ("parts", "region")),
            P(("parts", "region"), None, None),
            P(("parts", "region")),
            P(("parts", "region")),
            P(None, ("parts", "region")),
            P(None, None, "feat"),
            P(None, None, "feat"),
            P(None, None, "feat"),
            P(None, "feat"),
            P(None, "feat", None),
            P(),
            P(None, None, "feat"),
            P(None, None, "feat"),
            P(None, "feat"),
            P(None, "feat", None),
            P(),
            P(),
            P(),
        ),
        out_specs=(P(("parts", "region"), "feat"), P(("parts", "region"), "feat")),
        check_vma=False,
    )
```

profile of v0, /device:TPU:0, one launch (start us, length us, event | category | flops | bytes accessed | tf_op | source)
XLA Modules:
  0.0 493.2 jit_solution(5290544356450574259)
XLA Ops:
  15.9 6.3 %all-to-all-start = ((bf16[4,4,16384]{2,1,0:T(4,128)(2,1)}), bf16[4,4,16384]{2,1,0:T(4,128)(2,1)S(1)}, u32[]{:S(2)}, u32[]{:S(2)}) async-start(bf16[4,4,16384]{2,1,0:T(4,128)(2,1)} %reshape.43), calls=%async_computation | async-start | bytes 1048576 | tf_op jit(solution)/shard_map/all_to_all | solution.py:151
  23.6 13.1 %all-to-all-done = bf16[4,4,16384]{2,1,0:T(4,128)(2,1)S(1)} async-done(((bf16[4,4,16384]{2,1,0:T(4,128)(2,1)}), bf16[4,4,16384]{2,1,0:T(4,128)(2,1)S(1)}, u32[]{:S(2)}, u32[]{:S(2)}) %all-to-all-start) | async-done | bytes 524320 | tf_op jit(solution)/shard_map/all_to_all | solution.py:151
  37.3 170.3 %while.26 = (s32[]{:T(128)}, f32[512,128]{1,0:T(8,128)}, f32[512]{0:T(512)S(1)}, s32[8]{0:T(128)S(1)}, s32[16384]{0:T(1024)}, /*index=5*/s32[16384]{0:T(1024)}, ...) while((s32[]{:T(128)}, f32[512,128]{1,0:T(8,128)}, ...), condition=%wide.region_2.3_spmd.clone, body=%wide.region_0.2_spmd.clone.sunk | while | flops 826941952 | bytes 7711434 | solution.py:62
  44.9 6.2 %gather_fusion = bf16[2048,128]{1,0:T(8,128)(2,1)S(1)} fusion(bf16[2048,128]{1,0:T(8,128)(2,1)S(1)} %get-tuple-element.508, s32[2048]{0:T(1024)S(1)} %fusion.125), kind=kCustom, calls=%fused_computation.clone.clone.1 | custom fusion | bytes 1056768 | tf_op jit(solution)/shard_map/while/body/eval_jaxpr/gather | solution.py:46
  51.1 4.3 multiply_convert_fusion.6
  66.2 6.2 %gather_fusion = bf16[2048,128]{1,0:T(8,128)(2,1)S(1)} fusion(bf16[2048,128]{1,0:T(8,128)(2,1)S(1)} %get-tuple-element.508, s32[2048]{0:T(1024)S(1)} %fusion.125), kind=kCustom, calls=%fused_computation.clone.clone.1 | custom fusion | bytes 1056768 | tf_op jit(solution)/shard_map/while/body/eval_jaxpr/gather | solution.py:46
  72.4 4.3 multiply_convert_fusion.6
  87.5 6.2 %gather_fusion = bf16[2048,128]{1,0:T(8,128)(2,1)S(1)} fusion(bf16[2048,128]{1,0:T(8,128)(2,1)S(1)} %get-tuple-element.508, s32[2048]{0:T(1024)S(1)} %fusion.125), kind=kCustom, calls=%fused_computation.clone.clone.1 | custom fusion | bytes 1056768 | tf_op jit(solution)/shard_map/while/body/eval_jaxpr/gather | solution.py:46
  93.7 4.3 multiply_convert_fusion.6
  108.8 6.2 %gather_fusion = bf16[2048,128]{1,0:T(8,128)(2,1)S(1)} fusion(bf16[2048,128]{1,0:T(8,128)(2,1)S(1)} %get-tuple-element.508, s32[2048]{0:T(1024)S(1)} %fusion.125), kind=kCustom, calls=%fused_computation.clone.clone.1 | custom fusion | bytes 1056768 | tf_op jit(solution)/shard_map/while/body/eval_jaxpr/gather | solution.py:46
  115.0 4.3 multiply_convert_fusion.6
  130.1 6.2 %gather_fusion = bf16[2048,128]{1,0:T(8,128)(2,1)S(1)} fusion(bf16[2048,128]{1,0:T(8,128)(2,1)S(1)} %get-tuple-element.508, s32[2048]{0:T(1024)S(1)} %fusion.125), kind=kCustom, calls=%fused_computation.clone.clone.1 | custom fusion | bytes 1056768 | tf_op jit(solution)/shard_map/while/body/eval_jaxpr/gather | solution.py:46
  136.3 4.3 multiply_convert_fusion.6
  151.4 6.2 %gather_fusion = bf16[2048,128]{1,0:T(8,128)(2,1)S(1)} fusion(bf16[2048,128]{1,0:T(8,128)(2,1)S(1)} %get-tuple-element.508, s32[2048]{0:T(1024)S(1)} %fusion.125), kind=kCustom, calls=%fused_computation.clone.clone.1 | custom fusion | bytes 1056768 | tf_op jit(solution)/shard_map/while/body/eval_jaxpr/gather | solution.py:46
  157.6 4.3 multiply_convert_fusion.6
  172.7 6.2 %gather_fusion = bf16[2048,128]{1,0:T(8,128)(2,1)S(1)} fusion(bf16[2048,128]{1,0:T(8,128)(2,1)S(1)} %get-tuple-element.508, s32[2048]{0:T(1024)S(1)} %fusion.125), kind=kCustom, calls=%fused_computation.clone.clone.1 | custom fusion | bytes 1056768 | tf_op jit(solution)/shard_map/while/body/eval_jaxpr/gather | solution.py:46
  178.9 4.3 multiply_convert_fusion.6
  194.0 6.2 %gather_fusion = bf16[2048,128]{1,0:T(8,128)(2,1)S(1)} fusion(bf16[2048,128]{1,0:T(8,128)(2,1)S(1)} %get-tuple-element.508, s32[2048]{0:T(1024)S(1)} %fusion.125), kind=kCustom, calls=%fused_computation.clone.clone.1 | custom fusion | bytes 1056768 | tf_op jit(solution)/shard_map/while/body/eval_jaxpr/gather | solution.py:46
  211.7 30.5 %all-reduce.5.cloned.1.call-done = bf16[512,512]{1,0:T(8,128)(2,1)} async-done(((bf16[512,512]{1,0:T(8,128)(2,1)}), bf16[512,512]{1,0:T(8,128)(2,1)}) %all-reduce.5.cloned.1.call-update) | async-done | bytes 524304 | tf_op jit(solution)/shard_map/psum | solution.py:85
  244.7 66.5 %gather_fusion.2 = s32[8192]{0:T(1024)S(1)} fusion(s32[4,128]{1,0:T(4,128)S(1)} %bitcast.96, s32[8192]{0:T(1024)S(1)} %fusion.80), kind=kCustom, calls=%fused_computation.2 | custom fusion | bytes 131072 | tf_op jit(solution)/shard_map/gather | solution.py:163
  316.6 15.0 %all_gather.3 = bf16[2048,128]{1,0:T(8,128)(2,1)S(1)} all-gather(bf16[512,128]{1,0:T(8,128)(2,1)S(1)} %convolution_convert_fusion.6), channel_id=1, replica_groups=mesh['parts'=2,'region'=4,'feat'=4] {'region'}, dimensions={0}, use_global_device_ids=true | all-gather | bytes 655360 | tf_op jit(solution)/shard_map/all_gather | solution.py:159
  331.6 78.8 %while.27 = (s32[]{:T(128)}, f32[512,128]{1,0:T(8,128)}, f32[512]{0:T(512)S(1)}, s32[4]{0:T(128)S(1)}, s32[8192]{0:T(1024)}, /*index=5*/s32[8192]{0:T(1024)S(1)}...) while((s32[]{:T(128)}, f32[512,128]{1,0:T(8,128)}, ...), condition=%wide.region_9.10_spmd.clone, body=%wide.region_7.9_spmd.clone.sunk | while | flops 826941952 | bytes 9808826 | solution.py:62
  337.6 6.2 %gather_fusion.1 = bf16[2048,128]{1,0:T(8,128)(2,1)S(1)} fusion(bf16[2048,128]{1,0:T(8,128)(2,1)S(1)} %get-tuple-element.550, s32[2048]{0:T(1024)S(1)} %fusion.132), kind=kCustom, calls=%fused_computation.1.clone.clone.1 | custom fusion | bytes 1056768 | tf_op jit(solution)/shard_map/while/body/eval_jaxpr/gather | solution.py:46
  343.8 4.3 multiply_convert_fusion.7
  357.3 6.2 %gather_fusion.1 = bf16[2048,128]{1,0:T(8,128)(2,1)S(1)} fusion(bf16[2048,128]{1,0:T(8,128)(2,1)S(1)} %get-tuple-element.550, s32[2048]{0:T(1024)S(1)} %fusion.132), kind=kCustom, calls=%fused_computation.1.clone.clone.1 | custom fusion | bytes 1056768 | tf_op jit(solution)/shard_map/while/body/eval_jaxpr/gather | solution.py:46
  363.5 4.3 multiply_convert_fusion.7
  377.0 6.2 %gather_fusion.1 = bf16[2048,128]{1,0:T(8,128)(2,1)S(1)} fusion(bf16[2048,128]{1,0:T(8,128)(2,1)S(1)} %get-tuple-element.550, s32[2048]{0:T(1024)S(1)} %fusion.132), kind=kCustom, calls=%fused_computation.1.clone.clone.1 | custom fusion | bytes 1056768 | tf_op jit(solution)/shard_map/while/body/eval_jaxpr/gather | solution.py:46
  383.2 4.3 multiply_convert_fusion.7
  396.7 6.2 %gather_fusion.1 = bf16[2048,128]{1,0:T(8,128)(2,1)S(1)} fusion(bf16[2048,128]{1,0:T(8,128)(2,1)S(1)} %get-tuple-element.550, s32[2048]{0:T(1024)S(1)} %fusion.132), kind=kCustom, calls=%fused_computation.1.clone.clone.1 | custom fusion | bytes 1056768 | tf_op jit(solution)/shard_map/while/body/eval_jaxpr/gather | solution.py:46
  402.9 4.3 multiply_convert_fusion.7
  414.0 32.7 %all-reduce.9.cloned.1.call-done = bf16[512,512]{1,0:T(8,128)(2,1)} async-done(((bf16[512,512]{1,0:T(8,128)(2,1)}), bf16[512,512]{1,0:T(8,128)(2,1)}) %all-reduce.9.cloned.1.call-update) | async-done | bytes 524304 | tf_op jit(solution)/shard_map/psum | solution.py:85
  449.2 33.2 %all-reduce.11.cloned.1.call-done = bf16[512,512]{1,0:T(8,128)(2,1)} async-done(((bf16[512,512]{1,0:T(8,128)(2,1)}), bf16[512,512]{1,0:T(8,128)(2,1)}) %all-reduce.11.cloned.1.call-update) | async-done | bytes 524304 | tf_op jit(solution)/shard_map/psum | solution.py:97
  (216 shorter events, 136.6 us)
Async XLA Ops:
  7.2 5.3 %copy-start.16 = (s32[1,4,4]{2,1,0:T(4,128)S(1)}, s32[1,4,4]{2,1,0:T(4,128)}, u32[]{:S(2)}) copy-start(s32[1,4,4]{2,1,0:T(4,128)} %param.29) | copy-start | bytes 196
  11.2 11.1 %copy-start.3 = (bf16[512,512]{1,0:T(8,128)(2,1)S(1)}, bf16[512,512]{1,0:T(8,128)(2,1)}, u32[]{:S(2)}) copy-start(bf16[512,512]{1,0:T(8,128)(2,1)} %param.28) | copy-start | bytes 1572868
  11.2 11.1 %copy-start.5 = (bf16[2,512,128]{2,1,0:T(8,128)(2,1)S(1)}, bf16[2,512,128]{2,1,0:T(8,128)(2,1)}, u32[]{:S(2)}) copy-start(bf16[2,512,128]{2,1,0:T(8,128)(2,1)} %param.38) | copy-start | bytes 786436
  13.8 9.7 %copy-start.11 = (f32[2,4,128]{2,1,0:T(4,128)S(1)}, f32[2,4,128]{2,1,0:T(4,128)}, u32[]{:S(2)}) copy-start(f32[2,4,128]{2,1,0:T(4,128)} %param.39) | copy-start | bytes 12292
  13.8 9.7 %copy-start.17 = (f32[2,128]{1,0:T(2,128)S(1)}, f32[2,128]{1,0:T(2,128)}, u32[]{:S(2)}) copy-start(f32[2,128]{1,0:T(2,128)} %param.40) | copy-start | bytes 3076
  13.8 9.7 %copy-start.12 = (f32[2,512]{1,0:T(2,128)S(1)}, f32[2,512]{1,0:T(2,128)}, u32[]{:S(2)}) copy-start(f32[2,512]{1,0:T(2,128)} %param.42) | copy-start | bytes 12292
  13.8 9.7 %copy-start.13 = (f32[2,512]{1,0:T(2,128)S(1)}, f32[2,512]{1,0:T(2,128)}, u32[]{:S(2)}) copy-start(f32[2,512]{1,0:T(2,128)} %param.47) | copy-start | bytes 12292
  13.8 9.8 %copy-start.14 = (f32[2,512]{1,0:T(2,128)S(1)}, f32[2,512]{1,0:T(2,128)}, u32[]{:S(2)}) copy-start(f32[2,512]{1,0:T(2,128)} %param.48) | copy-start | bytes 12292
  13.8 9.8 %copy-start.15 = (f32[2,512]{1,0:T(2,128)S(1)}, f32[2,512]{1,0:T(2,128)}, u32[]{:S(2)}) copy-start(f32[2,512]{1,0:T(2,128)} %param.49) | copy-start | bytes 12292
  13.8 9.8 %copy-start.10 = (s32[8192]{0:T(1024)S(1)}, s32[8192]{0:T(1024)}, u32[]{:S(2)}) copy-start(s32[8192]{0:T(1024)} %param.34) | copy-start | bytes 98308
  15.9 20.8 %all-to-all-start = ((bf16[4,4,16384]{2,1,0:T(4,128)(2,1)}), bf16[4,4,16384]{2,1,0:T(4,128)(2,1)S(1)}, u32[]{:S(2)}, u32[]{:S(2)}) async-start(bf16[4,4,16384]{2,1,0:T(4,128)(2,1)} %reshape.43), calls=%async_computation | async-start | bytes 1048576 | tf_op jit(solution)/shard_map/all_to_all | solution.py:151
  22.2 220.0 %all-reduce.5.cloned.1.call-start = ((), (), s32[]{:S(2)}) async-start(), calls=%async_computation.1 | async-start | bytes 1048576 | tf_op jit(solution)/shard_map/psum | solution.py:85
  37.3 172.6 %copy-start.18 = (f32[2,128]{1,0:T(2,128)S(1)}, f32[2,128]{1,0:T(2,128)}, u32[]{:S(2)}) copy-start(f32[2,128]{1,0:T(2,128)} %param.45) | copy-start | bytes 3076
  207.6 34.6 %copy-start.20 = (bf16[2,128,512]{2,1,0:T(8,128)(2,1)S(1)}, bf16[2,128,512]{2,1,0:T(8,128)(2,1)}, u32[]{:S(2)}) copy-start(bf16[2,128,512]{2,1,0:T(8,128)(2,1)} %param.46) | copy-start | bytes 786436
  207.6 34.6 %copy-start.22 = (bf16[2,512,128]{2,1,0:T(8,128)(2,1)S(1)}, bf16[2,512,128]{2,1,0:T(8,128)(2,1)}, u32[]{:S(2)}) copy-start(bf16[2,512,128]{2,1,0:T(8,128)(2,1)} %param.44) | copy-start | bytes 786436
  209.8 34.9 %copy-start.1 = (s32[1,4,128]{2,1,0:T(4,128)S(1)}, s32[1,4,128]{2,1,0:T(4,128)}, u32[]{:S(2)}) copy-start(s32[1,4,128]{2,1,0:T(4,128)} %param.33) | copy-start | bytes 6148
  209.8 101.5 %all-reduce.7.cloned.1.call-start = ((), (), s32[]{:S(2)}) async-start(), calls=%async_computation.2 | async-start | bytes 1048576 | tf_op jit(solution)/shard_map/psum | solution.py:97
  244.6 202.0 %all-reduce.9.cloned.1.call-start = ((), (), s32[]{:S(2)}) async-start(), calls=%async_computation.3 | async-start | bytes 1048576 | tf_op jit(solution)/shard_map/psum | solution.py:85
  244.7 69.2 %copy-start.4 = (bf16[512,512]{1,0:T(8,128)(2,1)S(1)}, bf16[512,512]{1,0:T(8,128)(2,1)}, u32[]{:S(2)}) copy-start(bf16[512,512]{1,0:T(8,128)(2,1)} %param.28) | copy-start | bytes 1572868
  331.6 78.9 %copy-start.6 = (bf16[2,128,512]{2,1,0:T(8,128)(2,1)S(1)}, bf16[2,128,512]{2,1,0:T(8,128)(2,1)}, u32[]{:S(2)}) copy-start(bf16[2,128,512]{2,1,0:T(8,128)(2,1)} %param.41) | copy-start | bytes 786436
  331.6 6.0 %copy-start.7 = (bf16[512,256]{1,0:T(8,128)(2,1)}, bf16[512,256]{1,0:T(8,128)(2,1)S(1)}, u32[]{:S(2)}) copy-start(bf16[512,256]{1,0:T(8,128)(2,1)S(1)} %get-tuple-element.551) | copy-start | bytes 786436 | tf_op jit(solution)/shard_map/while
  331.6 6.0 %copy-start.24 = (s32[4]{0:T(128)}, s32[4]{0:T(128)S(1)}, u32[]{:S(2)}) copy-start(s32[4]{0:T(128)S(1)} %get-tuple-element.547) | copy-start | bytes 52 | tf_op jit(solution)/shard_map/while
  351.2 6.0 %copy-start.7 = (bf16[512,256]{1,0:T(8,128)(2,1)}, bf16[512,256]{1,0:T(8,128)(2,1)S(1)}, u32[]{:S(2)}) copy-start(bf16[512,256]{1,0:T(8,128)(2,1)S(1)} %get-tuple-element.551) | copy-start | bytes 786436 | tf_op jit(solution)/shard_map/while
  351.3 6.0 %copy-start.24 = (s32[4]{0:T(128)}, s32[4]{0:T(128)S(1)}, u32[]{:S(2)}) copy-start(s32[4]{0:T(128)S(1)} %get-tuple-element.547) | copy-start | bytes 52 | tf_op jit(solution)/shard_map/while
  371.0 6.0 %copy-start.7 = (bf16[512,256]{1,0:T(8,128)(2,1)}, bf16[512,256]{1,0:T(8,128)(2,1)S(1)}, u32[]{:S(2)}) copy-start(bf16[512,256]{1,0:T(8,128)(2,1)S(1)} %get-tuple-element.551) | copy-start | bytes 786436 | tf_op jit(solution)/shard_map/while
  371.0 6.0 %copy-start.24 = (s32[4]{0:T(128)}, s32[4]{0:T(128)S(1)}, u32[]{:S(2)}) copy-start(s32[4]{0:T(128)S(1)} %get-tuple-element.547) | copy-start | bytes 52 | tf_op jit(solution)/shard_map/while
  390.7 6.0 %copy-start.7 = (bf16[512,256]{1,0:T(8,128)(2,1)}, bf16[512,256]{1,0:T(8,128)(2,1)S(1)}, u32[]{:S(2)}) copy-start(bf16[512,256]{1,0:T(8,128)(2,1)S(1)} %get-tuple-element.551) | copy-start | bytes 786436 | tf_op jit(solution)/shard_map/while
  390.7 6.0 %copy-start.24 = (s32[4]{0:T(128)}, s32[4]{0:T(128)S(1)}, u32[]{:S(2)}) copy-start(s32[4]{0:T(128)S(1)} %get-tuple-element.547) | copy-start | bytes 52 | tf_op jit(solution)/shard_map/while
  410.4 36.2 %copy-start.19 = (f32[128]{0:T(128)S(1)}, f32[128]{0:T(128)}, u32[]{:S(2)}) copy-start(f32[128]{0:T(128)} %get-tuple-element.336) | copy-start | bytes 1540
  410.4 36.2 %copy-start.21 = (bf16[2,128,512]{2,1,0:T(8,128)(2,1)S(1)}, bf16[2,128,512]{2,1,0:T(8,128)(2,1)}, u32[]{:S(2)}) copy-start(bf16[2,128,512]{2,1,0:T(8,128)(2,1)} %param.46) | copy-start | bytes 786436
  410.4 36.2 %copy-start.23 = (bf16[2,512,128]{2,1,0:T(8,128)(2,1)S(1)}, bf16[2,512,128]{2,1,0:T(8,128)(2,1)}, u32[]{:S(2)}) copy-start(bf16[2,512,128]{2,1,0:T(8,128)(2,1)} %param.44) | copy-start | bytes 786436
  412.6 69.8 %all-reduce.11.cloned.1.call-start = ((), (), s32[]{:S(2)}) async-start(), calls=%async_computation.4 | async-start | bytes 1048576 | tf_op jit(solution)/shard_map/psum | solution.py:97
  (11 other events, 32.5 us)
Sparse Core Ops, SparseCore 0:
  209.9 32.2 all-reduce.4
  244.7 33.1 all-reduce.6
  412.7 33.9 all-reduce.8
  449.2 33.1 all-reduce.10
where the time goes:
time: 496 us; the launch traced here: 493 us
  local copies, waits for them, and re-layouts  165 us (33%)
  matrix products  138 us (28%)
  waiting for transfers between devices  110 us (22%)
  loops' own time  23.4 us (5%)
  other arithmetic  21 us (4%)
  blocking collectives  15 us (3%)
  between operations  14.2 us (3%)
  starting transfers between devices  6.46 us (1%)
    gather x12, local copies, waits for them, and re-layouts, visit_block(): summed = lookup[send_part].astype(jnp.float32) + recv_rows  74.2 us
    gather x1, local copies, waits for them, and re-layouts, per_device(): row_index = wanted[source, m2m_sender % capacity]  66.5 us
    psum x2, waiting for transfers between devices, node_step(): lax.psum(partial_agg.astype(jnp.bfloat16), 'feat').astype(jnp.float32)  63.2 us
    dot_general x12, matrix products, visit_block(): jnp.einsum('ke,kh->eh', feat_part, w_feat, precision=lax.Precision.HIGHEST)  51.8 us
    dot_general x12, matrix products, visit_block(): lax.dot_general(member, recv_pair, (((0,), (0,)), ((), ())), preferred_el...  38.9 us
    psum x2, waiting for transfers between devices, node_step(): lax.psum(partial_update.astype(jnp.bfloat16), 'feat').astype(jnp.float32)  33.2 us
    dot_general x12, matrix products, visit_block(): jnp.dot(member, hidden, preferred_element_type=jnp.float32)  31.5 us
    another operation x2, loops' own time, edge_sums(): result, unused = lax.scan(visit_block, initial, starts)  23.4 us
  transfers between devices with their start and end apart: 5, of which 4 were waited for; matrix products, arithmetic and copies ran while one was open for 14% of the time, Pallas kernels for 0%

commit v1 on v0

--- a/solution.py
+++ b/solution.py
@@ -1,6 +1,10 @@
+import functools
+
 import jax
 import jax.numpy as jnp
 from jax import lax
+from jax.experimental import pallas as pl
+from jax.experimental.pallas import tpu as pltpu
 from jax.sharding import PartitionSpec as P
 
 TILE = 128
@@ -175,9 +179,356 @@
     )
 
 
+MESH = pl.DeviceIdType.MESH
+BF = jnp.bfloat16
+F32 = jnp.float32
+
+
+def dot_dims(left, right, left_dim, right_dim):
+    return lax.dot_general(
+        left, right, (((left_dim,), (right_dim,)), ((), ())), preferred_element_type=F32
+    )
+
+
+def one_hot(row, count):
+    ids = lax.broadcasted_iota(jnp.int32, (count, row.shape[1]), 0)
+    return jnp.where(ids == row, 1.0, 0.0).astype(BF)
+
+
+def swish_tanh(value):
+    half = 0.5 * value
+    return half + half * jnp.tanh(half)
+
+
+def fused(
+    regions, feats,
+    grid_ref, mesh_ref, tiles_ref, gs_ref, gr_ref, gf_ref, mt_ref, ms_ref, mr_ref, mf_ref,
+    w_send, w_recv, w_ef, b_edge, weo_ref, beo, wself_ref, wagg_ref, bnode_ref, wno_ref, bno,
+    gain, shift,
+    out_enc, out_proc,
+    proj, stage, tab, table_all, recv_tab, acc, cols,
+    weo, wno, wself, wagg, bnode, sum_stage, sum_all, cnt_stage, enc, stage2, tab2, fold2,
+    proc_stage, proc_all,
+    tile_send, tile_recv, id_send, id_recv, w_ssem, w_rsem, b_ssem, b_rsem, s_ssem, s_rsem,
+    e_ssem, e_rsem, m_ssem, m_rsem, p_ssem, p_rsem,
+):
+    reg = lax.axis_index("region")
+    ft = lax.axis_index("feat")
+    width = w_send.shape[2]
+    nodes = mesh_ref.shape[0]
+    slots = tab.shape[2]
+    rows = nodes // feats
+    core = ft % 2
+    across = (ft + 2) % feats
+    partner = ft - core + (1 - core)
+
+    barrier = pltpu.get_barrier_semaphore()
+    for off in range(1, regions):
+        pl.semaphore_signal(
+            barrier, inc=1, device_id={"region": (reg + off) % regions}, device_id_type=MESH
+        )
+    for off in range(1, feats):
+        pl.semaphore_signal(
+            barrier, inc=1, device_id={"feat": (ft + off) % feats}, device_id_type=MESH
+        )
+    pl.semaphore_wait(barrier, regions + feats - 2)
+
+    def remote(source, target, send, recv, axis, index):
+        return pltpu.make_async_remote_copy(
+            src_ref=source, dst_ref=target, send_sem=send, recv_sem=recv,
+            device_id={axis: index}, device_id_type=MESH,
+        )
+
+    def to_peers(axis, me, count, source_of, target_of, send, recv):
+        copies = []
+        for off in range(1, count):
+            peer = (me + off) % count
+            copies.append(
+                remote(source_of(peer), target_of(me), send.at[off - 1], recv.at[off - 1], axis, peer)
+            )
+        return copies
+
+    id_copies = to_peers(
+        "region", reg, regions, lambda p: mt_ref.at[0], lambda m: table_all.at[m], id_send, id_recv
+    )
+    bias_copies = to_peers(
+        "feat", ft, feats, lambda p: bnode_ref, lambda m: bnode.at[m], b_ssem, b_rsem
+    )
+    kinds = ((weo_ref, weo), (wself_ref, wself), (wagg_ref, wagg), (wno_ref, wno))
+
+    def weight_copies(layer, route):
+        copies = []
+        for kind, (own, full) in enumerate(kinds):
+            slot = across if route == 2 else ft
+            source = full.at[layer, slot] if route == 2 else own.at[layer]
+            copies.append(
+                remote(
+                    source, full.at[layer, slot],
+                    w_ssem.at[layer, route, kind], w_rsem.at[layer, route, kind],
+                    "feat", across if route == 0 else partner,
+                )
+            )
+        return copies
+
+    first_hops = [[weight_copies(layer, route) for route in range(2)] for layer in range(2)]
+    forwards = [weight_copies(layer, 2) for layer in range(2)]
+    for copy in id_copies + bias_copies:
+        copy.start()
+
+    @pl.loop(0, grid_ref.shape[0] // 512)
+    def project(step):
+        block = dot_dims(w_send[0], grid_ref[pl.ds(step * 512, 512), :], 0, 1).astype(BF)
+        for part in range(512 // TILE):
+            proj[step * (512 // TILE) + part] = block[:, part * TILE : (part + 1) * TILE]
+
+    cap = slots // TILE
+    for target in range(regions):
+        for slot in range(cap):
+            tile = jnp.maximum(tiles_ref[0, target, slot], 0)
+            stage[target, :, slot * TILE : (slot + 1) * TILE] = proj[tile]
+    tile_copies = to_peers(
+        "region", reg, regions, lambda p: stage.at[p], lambda m: tab.at[m], tile_send, tile_recv
+    )
+    for copy in tile_copies:
+        copy.start()
+    for layer in range(2):
+        for route in range(2):
+            for copy in first_hops[layer][route]:
+                copy.start()
+    tab[reg] = stage[reg]
+    table_all[reg] = mt_ref[0]
+    bnode[ft] = bnode_ref[...]
+    for layer in range(2):
+        for own, full in kinds:
+            full[layer, ft] = own[layer]
+
+    half_nodes = nodes // 2
+
+    def set_receivers(layer, latent):
+        base = jnp.concatenate(
+            [w_ef[layer], b_edge[layer : layer + 1], jnp.zeros((3, width), F32)], axis=0
+        )
+        turned = jnp.concatenate([base] * (width // 8), axis=0).T
+        cols[...] = turned
+        table = dot_dims(w_recv[layer], latent, 0, 1) + turned[:, 4:5]
+        table = table.astype(BF)
+        recv_tab[0:width] = table[:, :half_nodes]
+        recv_tab[width:] = table[:, half_nodes:]
+        acc[...] = jnp.zeros_like(acc)
+
+    def edge_block(at, size, s_ref, r_ref, f_ref, table, shift_by):
+        here = pl.ds(pl.multiple_of(at, size), size)
+        send = s_ref[:, here]
+        recv = r_ref[:, here]
+        upper = recv >= half_nodes
+        low = jnp.where(upper, recv - half_nodes, recv)
+        picks = one_hot(low, half_nodes)
+        found = jnp.dot(recv_tab[...], picks, preferred_element_type=F32)
+        value = jnp.where(upper, found[width:], found[:width])
+        source = send >> shift_by
+        local = send & ((1 << shift_by) - 1)
+        found = jnp.dot(table, one_hot(local, 1 << shift_by), preferred_element_type=F32)
+        chosen = found[:width]
+        for part in range(1, table.shape[0] // width):
+            chosen = jnp.where(source == part, found[part * width : (part + 1) * width], chosen)
+        value = value + chosen
+        for k in range(4):
+            value = value + cols[:, k : k + 1] * f_ref[k : k + 1, here]
+        hidden = swish_tanh(value)
+        ids = lax.broadcasted_iota(jnp.int32, (16, size), 0)
+        side = jnp.where(upper, 1, 0)
+        spread = jnp.concatenate(
+            [
+                jnp.where(upper, 0.0, hidden).astype(BF),
+                jnp.where(upper, hidden, 0.0).astype(BF),
+                jnp.where(ids == side, 1.0, 0.0).astype(BF),
+            ],
+            axis=0,
+        )
+        acc[...] += dot_dims(spread, picks, 1, 1)
+
+    def share_sums(layer):
+        for owner in range(feats):
+            side = (owner * rows) // half_nodes
+            lane = (owner * rows) % half_nodes
+            sum_stage[layer, owner] = acc[
+                side * width : (side + 1) * width, lane : lane + rows
+            ].astype(BF)
+            cnt_stage[owner] = acc[2 * width + side : 2 * width + side + 1, lane : lane + rows]
+        copies = to_peers(
+            "feat", ft, feats, lambda p: sum_stage.at[layer, p], lambda m: sum_all.at[layer, m],
+            s_ssem.at[layer], s_rsem.at[layer],
+        )
+        for copy in copies:
+            copy.start()
+        sum_all[layer, ft] = sum_stage[layer, ft]
+        return copies
+
+    def node_rows(layer, latent):
+        sums = sum_all[layer].reshape(feats * width, rows)
+        agg = dot_dims(sums, weo[layer].reshape(feats * width, -1), 0, 0)
+        count = jnp.broadcast_to(cnt_stage[ft], (rows, rows)).T
+        agg = agg + jnp.concatenate([count] * (agg.shape[1] // rows), axis=1) * beo[layer : layer + 1]
+        agg = agg.astype(BF)
+        update = bno[layer : layer + 1]
+        for part in range(feats):
+            pre = jnp.dot(latent, wself[layer, part], preferred_element_type=F32)
+            pre = pre + jnp.dot(agg, wagg[layer, part], preferred_element_type=F32)
+            hidden = swish_tanh(pre + bnode[part, layer : layer + 1]).astype(BF)
+            update = update + jnp.dot(hidden, wno[layer, part], preferred_element_type=F32)
+        normed = layer_norm(update, gain[layer : layer + 1], shift[layer : layer + 1])
+        return (latent.astype(F32) + normed).astype(BF)
+
+    set_receivers(0, mesh_ref[...])
+    for copy in tile_copies:
+        copy.wait()
+    size = 512
+    steps = gs_ref.shape[1] // size
+    shift_first = slots.bit_length() - 1
+
+    @pl.loop(0, steps // 2)
+    def first_half(step):
+        edge_block(step * size, size, gs_ref, gr_ref, gf_ref, tab[...].reshape(regions * width, slots), shift_first)
+
+    for copy in first_hops[0][0]:
+        copy.wait_recv()
+    for copy in forwards[0]:
+        copy.start()
+
+    @pl.loop(steps // 2, steps)
+    def second_half(step):
+        edge_block(step * size, size, gs_ref, gr_ref, gf_ref, tab[...].reshape(regions * width, slots), shift_first)
+
+    sums = share_sums(0)
+    for copy in first_hops[0][1] + forwards[0] + sums + bias_copies:
+        copy.wait()
+    for copy in first_hops[1][0]:
+        copy.wait_recv()
+    for copy in forwards[1]:
+        copy.start()
+    mine = pl.ds(pl.multiple_of(ft * rows, rows), rows)
+    enc[ft] = node_rows(0, mesh_ref[mine, :])
+    enc_copies = to_peers(
+        "feat", ft, feats, lambda p: enc.at[ft], lambda m: enc.at[m], e_ssem, e_rsem
+    )
+    for copy in enc_copies:
+        copy.start()
+    for copy in id_copies + enc_copies:
+        copy.wait()
+    whole = enc[...].reshape(nodes, -1)
+    sent = dot_dims(w_send[1], whole, 0, 1).astype(BF)
+    for target in range(regions):
+        wanted = table_all[target, pl.ds(reg, 1), :]
+        stage2[target] = jnp.dot(sent, one_hot(wanted, nodes), preferred_element_type=F32).astype(BF)
+    row_copies = to_peers(
+        "region", reg, regions, lambda p: stage2.at[p], lambda m: tab2.at[m], m_ssem, m_rsem
+    )
+    for copy in row_copies:
+        copy.start()
+    tab2[reg] = stage2[reg]
+    set_receivers(1, whole)
+    for owner in range(feats):
+        out_enc[owner * rows : (owner + 1) * rows, :] = enc[owner, :, pl.ds(pl.multiple_of(ft * width, width), width)]
+    for copy in row_copies:
+        copy.wait()
+    mcap = tab2.shape[2]
+    for part in range(regions):
+        fold2[
+            (part // 2) * width : (part // 2 + 1) * width, (part % 2) * mcap : (part % 2 + 1) * mcap
+        ] = tab2[part]
+    shift_second = (2 * mcap).bit_length() - 1
+
+    @pl.loop(0, ms_ref.shape[1] // size)
+    def mesh_steps(step):
+        edge_block(step * size, size, ms_ref, mr_ref, mf_ref, fold2[...], shift_second)
+
+    sums = share_sums(1)
+    for copy in first_hops[1][1] + forwards[1] + sums:
+        copy.wait()
+    for layer in range(2):
+        for copy in first_hops[layer][0]:
+            copy.wait_send()
+    result = node_rows(1, enc[ft])
+    for owner in range(feats):
+        proc_stage[owner] = result[:, owner * width : (owner + 1) * width]
+    proc_copies = to_peers(
+        "feat", ft, feats, lambda p: proc_stage.at[p], lambda m: proc_all.at[m], p_ssem, p_rsem
+    )
+    for copy in proc_copies:
+        copy.start()
+    proc_all[ft] = proc_stage[ft]
+    for copy in proc_copies:
+        copy.wait()
+    out_proc[...] = proc_all[...].reshape(nodes, width)
+
+
+def fused_device(regions, feats, *args):
+    (grid_latent, mesh_latent, send_tiles, gs, gr, gf, mt, ms, mr, mf, w_send) = args[:11]
+    nodes, latent = mesh_latent.shape
+    width = w_send.shape[2]
+    slots = send_tiles.shape[2] * TILE
+    mcap = mt.shape[2]
+    rows = nodes // feats
+    args = list(args)
+    for at in (3, 4, 7, 8):
+        args[at] = args[at].reshape(1, -1)
+    specs = [pl.BlockSpec(memory_space=pltpu.VMEM)] * len(args)
+    specs[2] = pl.BlockSpec(memory_space=pltpu.SMEM)
+    dma = pltpu.SemaphoreType.DMA
+    vm = pltpu.VMEM
+    return pl.pallas_call(
+        functools.partial(fused, regions, feats),
+        out_shape=(jax.ShapeDtypeStruct((nodes, width), BF),) * 2,
+        in_specs=specs,
+        out_specs=(pl.BlockSpec(memory_space=pltpu.VMEM),) * 2,
+        scratch_shapes=[
+            vm((grid_latent.shape[0] // TILE, width, TILE), BF),
+            vm((regions, width, slots), BF),
+            vm((regions, width, slots), BF),
+            vm((regions, regions, mcap), jnp.int32),
+            vm((2 * width, nodes // 2), BF),
+            vm((2 * width + 16, nodes // 2), F32),
+            vm((width, width), F32),
+            vm((2, feats, width, latent), BF),
+            vm((2, feats, width, latent), BF),
+            vm((2, feats, latent, width), BF),
+            vm((2, feats, latent, width), BF),
+            vm((feats, 2, width), F32),
+            vm((2, feats, width, rows), BF),
+            vm((2, feats, width, rows), BF),
+            vm((feats, 1, rows), F32),
+            vm((feats, rows, latent), BF),
+            vm((regions, width, mcap), BF),
+            vm((regions, width, mcap), BF),
+            vm((regions // 2 * width, 2 * mcap), BF),
+            vm((feats, rows, width), BF),
+            vm((feats, rows, width), BF),
+            dma((regions - 1,)), dma((regions - 1,)),
+            dma((regions - 1,)), dma((regions - 1,)),
+            dma((2, 3, 4)), dma((2, 3, 4)),
+            dma((feats - 1,)), dma((feats - 1,)),
+            dma((2, feats - 1)), dma((2, feats - 1)),
+            dma((feats - 1,)), dma((feats - 1,)),
+            dma((regions - 1,)), dma((regions - 1,)),
+            dma((feats - 1,)), dma((feats - 1,)),
+        ],
+        compiler_params=pltpu.CompilerParams(
+            collective_id=0, has_side_effects=True, vmem_limit_bytes=48 << 20
+        ),
+    )(*args)
+
+
+def pick_form(regions, feats, *args):
+    width = args[10].shape[2]
+    rows = args[1].shape[0] // feats
+    if feats == 4 and width == 128 and rows == 128 and regions % 2 == 0 and regions <= 8:
+        return fused_device(regions, feats, *args)
+    return per_device(*args)
+
+
 def solution(mesh):
     return jax.shard_map(
-        per_device,
+        functools.partial(pick_form, mesh.shape["region"], mesh.shape["feat"]),
         mesh=mesh,
         in_specs=(
             P(("parts", "region"), None),

time: 496 us -> 103 us (0.21)
  local copies, waits for them, and re-layouts: 165 us -> 20.8 us
  matrix products: 138 us -> 0 us
  waiting for transfers between devices: 110 us -> 0 us
  Pallas kernels: 0 us -> 80.5 us
  loops' own time: 23.4 us -> 0 us
  other arithmetic: 21 us -> 0 us
  blocking collectives: 15 us -> 0 us
  between operations: 14.2 us -> 0.68 us
  starting transfers between devices: 6.46 us -> 0 us
    gather x13 -> x0, local copies, waits for them, and re-layouts: 141 us -> none  [the longest x12 74.2 us: visit_block(): summed = lookup[send_part].astype(jnp.float32) + recv_rows]
    dot_general x47 -> x0, matrix products: 138 us -> none  [the longest x12 51.8 us: visit_block(): jnp.einsum('ke,kh->eh', feat_part, w_feat, precision=lax.Precision.HIGHEST)]
    psum x4 -> x0, waiting for transfers between devices: 96.4 us -> none  [the longest x2 63.2 us: node_step(): lax.psum(partial_agg.astype(jnp.bfloat16), 'feat').astype(jnp.float32)]
    pallas_call x0 -> x1, Pallas kernels: none -> 80.5 us  [fused_device(): pl.pallas_call(functools.partial(fused, regions, feats), out_shape=(jax.S...]
    another operation x2 -> x0, loops' own time: 23.4 us -> none  [edge_sums(): result, unused = lax.scan(visit_block, initial, starts)]
    unnamed x46 -> x48, local copies, waits for them, and re-layouts: 3.13 us -> 20.8 us
    dynamic_slice x26 -> x0, local copies, waits for them, and re-layouts: 16.9 us -> none  [the longest x12 9.44 us: visit_block(): recv_part = lax.dynamic_slice_in_dim(receivers, start, edge_block)]
    all_gather x1 -> x0, blocking collectives: 15 us -> none  [per_device(): everything = lax.all_gather(mesh_send, 'region', axis=0, tiled=True)]
  transfers between devices with their start and end apart: 5 -> 0, of which waited for: 4 -> 0; matrix products, arithmetic and copies ran while one was open for 14% -> 0% of each run, Pallas kernels for 0% -> 0%
where the time goes in v1:
time: 103 us; the launch traced here: 102 us
  Pallas kernels  80.5 us (78%)
  local copies, waits for them, and re-layouts  20.8 us (20%)
    pallas_call x1, Pallas kernels, fused_device(): pl.pallas_call(functools.partial(fused, regions, feats), out_shape=(jax.S...  80.5 us
    unnamed x48, local copies, waits for them, and re-layouts  20.8 us

profile of v1, /device:TPU:0, one launch (start us, length us, event | category | flops | bytes accessed | tf_op | source)
XLA Modules:
  0.0 102.0 jit_solution(9779890740517819607)
XLA Ops:
  0.6 0.0 copy-start
  0.6 1.6 %copy-done = bf16[2048,512]{1,0:T(8,128)(2,1)S(1)} copy-done((bf16[2048,512]{1,0:T(8,128)(2,1)S(1)}, bf16[2048,512]{1,0:T(8,128)(2,1)}, u32[]{:S(2)}) %copy-start) | copy-done | bytes 2097176
  2.2 0.0 copy-start.1
  2.2 1.0 %copy-done.1 = bf16[512,512]{1,0:T(8,128)(2,1)S(1)} copy-done((bf16[512,512]{1,0:T(8,128)(2,1)S(1)}, bf16[512,512]{1,0:T(8,128)(2,1)}, u32[]{:S(2)}) %copy-start.1) | copy-done | bytes 524312
  3.3 0.0 copy-start.2
  3.3 0.9 copy-done.2
  4.2 0.0 copy-start.3
  4.2 0.9 copy-done.3
  5.2 0.0 copy-start.4
  5.2 0.9 copy-done.4
  6.1 0.0 copy-start.5
  6.1 0.9 copy-done.5
  7.1 0.9 copy-done.6
  8.0 0.9 copy-done.7
  9.0 0.9 copy-done.8
  9.9 0.9 copy-done.9
  10.8 0.8 copy-done.10
  11.7 0.8 copy-done.11
  12.5 0.8 copy-done.12
  13.3 0.8 copy-done.13
  14.0 0.7 copy-done.14
  14.7 0.7 copy-done.15
  15.4 0.7 copy-done.16
  16.1 0.7 copy-done.17
  16.8 0.7 copy-done.18
  17.5 0.7 copy-done.19
  18.1 0.7 copy-done.20
  18.8 0.7 copy-done.21
  19.5 0.7 copy-done.22
  20.2 80.5 %shard_map.230 = (bf16[512,128]{1,0:T(8,128)(2,1)S(1)}, bf16[512,128]{1,0:T(8,128)(2,1)S(1)}) custom-call(bf16[2048,512]{1,0:T(8,128)(2,1)S(1)} %copy-done, bf16[512,512]{1,0:T(8,128)(2,1)S(1)} %copy-done.1, s32[1,4,4]{2,1,0:T(4,128)S(1)} %copy-done.19, s32[1,16384]{1,0:T(1,128)S(1)} %bitcast.4, s32[1,16384]{1,0:T(1,128)S(1)} %bitcast.5, ...), custom_call_target="tpu_custom_call" | custom-call | tf_op jit(solution)/shard_map/pallas_call | solution.py:479
  100.7 0.7 copy.27
  101.3 0.7 copy.28
  (17 shorter events, 0.0 us)
Async XLA Ops:
  0.6 1.6 %copy-start = (bf16[2048,512]{1,0:T(8,128)(2,1)S(1)}, bf16[2048,512]{1,0:T(8,128)(2,1)}, u32[]{:S(2)}) copy-start(bf16[2048,512]{1,0:T(8,128)(2,1)} %grid_ref.1) | copy-start | bytes 6291460
  2.2 1.0 %copy-start.1 = (bf16[512,512]{1,0:T(8,128)(2,1)S(1)}, bf16[512,512]{1,0:T(8,128)(2,1)}, u32[]{:S(2)}) copy-start(bf16[512,512]{1,0:T(8,128)(2,1)} %mesh_ref.1) | copy-start | bytes 1572868
  3.3 0.9 copy-start.2
  4.2 0.9 copy-start.3
  5.2 0.9 copy-start.4
  6.1 0.9 copy-start.5
  7.1 0.9 copy-start.6
  8.0 0.9 copy-start.7
  9.0 0.9 copy-start.8
  9.9 0.9 copy-start.9
  10.8 0.8 copy-start.10
  11.7 0.8 copy-start.11
  12.5 0.8 copy-start.12
  13.3 0.8 copy-start.13
  14.0 0.7 copy-start.14
  14.7 0.7 copy-start.15
  15.4 0.7 copy-start.16
  16.1 0.7 copy-start.17
  16.8 0.7 copy-start.18
  17.5 0.7 copy-start.19
  18.1 0.7 copy-start.20
  18.8 0.7 copy-start.21
  19.5 0.7 copy-start.22

commit v2 on v1

--- a/solution.py
+++ b/solution.py
@@ -181,6 +181,7 @@
 
 MESH = pl.DeviceIdType.MESH
 BF = jnp.bfloat16
+EDGE_BLOCK = 2048
 F32 = jnp.float32
 
 
@@ -202,13 +203,15 @@
 
 def fused(
     regions, feats,
-    grid_ref, mesh_ref, tiles_ref, gs_ref, gr_ref, gf_ref, mt_ref, ms_ref, mr_ref, mf_ref,
-    w_send, w_recv, w_ef, b_edge, weo_ref, beo, wself_ref, wagg_ref, bnode_ref, wno_ref, bno,
-    gain, shift,
+    grid_hbm, mesh_hbm, tiles_ref, gs_hbm, gr_hbm, gf_hbm, mt_hbm, ms_hbm, mr_hbm, mf_hbm,
+    w_send_hbm, w_recv_hbm, w_ef_hbm, b_edge_hbm, weo_ref, beo_hbm, wself_ref, wagg_ref, bnode_hbm,
+    wno_ref, bno_hbm, gain_hbm, shift_hbm,
     out_enc, out_proc,
     proj, stage, tab, table_all, recv_tab, acc, cols,
     weo, wno, wself, wagg, bnode, sum_stage, sum_all, cnt_stage, enc, stage2, tab2, fold2,
-    proc_stage, proc_all,
+    proc_stage, proc_all, send_picks, recv_picks, partial_sum,
+    grid_ref, w_send, mesh_ref, w_recv, w_ef, b_edge, gs_ref, gr_ref, gf_ref, mt_ref, ms_ref,
+    mr_ref, mf_ref, beo, bnode_ref, bno, gain, shift, in_sem, own_sem,
     tile_send, tile_recv, id_send, id_recv, w_ssem, w_rsem, b_ssem, b_rsem, s_ssem, s_rsem,
     e_ssem, e_rsem, m_ssem, m_rsem, p_ssem, p_rsem,
 ):
@@ -222,6 +225,20 @@
     across = (ft + 2) % feats
     partner = ft - core + (1 - core)
 
+    loads = [
+        pltpu.make_async_copy(source, target, in_sem.at[at])
+        for at, (source, target) in enumerate(
+            (
+                (w_send_hbm, w_send), (grid_hbm, grid_ref), (mesh_hbm, mesh_ref),
+                (w_recv_hbm, w_recv), (w_ef_hbm, w_ef), (b_edge_hbm, b_edge), (gs_hbm, gs_ref),
+                (gr_hbm, gr_ref), (gf_hbm, gf_ref), (mt_hbm, mt_ref), (bnode_hbm, bnode_ref),
+                (ms_hbm, ms_ref), (mr_hbm, mr_ref), (mf_hbm, mf_ref), (beo_hbm, beo),
+                (bno_hbm, bno), (gain_hbm, gain), (shift_hbm, shift),
+            )
+        )
+    ]
+    for load in loads:
+        load.start()
     barrier = pltpu.get_barrier_semaphore()
     for off in range(1, regions):
         pl.semaphore_signal(
@@ -272,8 +289,11 @@
 
     first_hops = [[weight_copies(layer, route) for route in range(2)] for layer in range(2)]
     forwards = [weight_copies(layer, 2) for layer in range(2)]
-    for copy in id_copies + bias_copies:
-        copy.start()
+    for route in range(2):
+        for copy in first_hops[0][route]:
+            copy.start()
+    for load in loads[:2]:
+        load.wait()
 
     @pl.loop(0, grid_ref.shape[0] // 512)
     def project(step):
@@ -291,16 +311,23 @@
     )
     for copy in tile_copies:
         copy.start()
-    for layer in range(2):
-        for route in range(2):
-            for copy in first_hops[layer][route]:
-                copy.start()
+    for load in loads[2:]:
+        load.wait()
+    for copy in id_copies + bias_copies:
+        copy.start()
+    for route in range(2):
+        for copy in first_hops[1][route]:
+            copy.start()
+    keeps = [
+        pltpu.make_async_copy(own.at[layer], full.at[layer, ft], own_sem.at[layer, kind])
+        for layer in range(2)
+        for kind, (own, full) in enumerate(kinds)
+    ]
+    for copy in keeps:
+        copy.start()
     tab[reg] = stage[reg]
     table_all[reg] = mt_ref[0]
     bnode[ft] = bnode_ref[...]
-    for layer in range(2):
-        for own, full in kinds:
-            full[layer, ft] = own[layer]
 
     half_nodes = nodes // 2
 
@@ -316,25 +343,33 @@
         recv_tab[width:] = table[:, half_nodes:]
         acc[...] = jnp.zeros_like(acc)
 
-    def edge_block(at, size, s_ref, r_ref, f_ref, table, shift_by):
-        here = pl.ds(pl.multiple_of(at, size), size)
-        send = s_ref[:, here]
+    def pick_edges(step, s_ref, r_ref, shift_by):
+        here = pl.ds(pl.multiple_of(step * size, size), size)
         recv = r_ref[:, here]
-        upper = recv >= half_nodes
-        low = jnp.where(upper, recv - half_nodes, recv)
-        picks = one_hot(low, half_nodes)
-        found = jnp.dot(recv_tab[...], picks, preferred_element_type=F32)
-        value = jnp.where(upper, found[width:], found[:width])
-        source = send >> shift_by
-        local = send & ((1 << shift_by) - 1)
-        found = jnp.dot(table, one_hot(local, 1 << shift_by), preferred_element_type=F32)
+        low = jnp.where(recv >= half_nodes, recv - half_nodes, recv)
+        recv_picks[step] = one_hot(low, half_nodes)
+        local = s_ref[:, here] & ((1 << shift_by) - 1)
+        send_picks[step, 0 : 1 << shift_by] = one_hot(local, 1 << shift_by)
+
+    def start_edges(step, r_ref, f_ref):
+        here = pl.ds(pl.multiple_of(step * size, size), size)
+        found = jnp.dot(recv_tab[...], recv_picks[step], preferred_element_type=F32)
+        value = jnp.where(r_ref[:, here] >= half_nodes, found[width:], found[:width])
+        for k in range(4):
+            value = value + cols[:, k : k + 1] * f_ref[k : k + 1, here]
+        partial_sum[step] = value
+
+    def finish_edges(step, s_ref, r_ref, table, shift_by):
+        here = pl.ds(pl.multiple_of(step * size, size), size)
+        source = s_ref[:, here] >> shift_by
+        upper = r_ref[:, here] >= half_nodes
+        found = jnp.dot(
+            table, send_picks[step, 0 : 1 << shift_by], preferred_element_type=F32
+        )
         chosen = found[:width]
         for part in range(1, table.shape[0] // width):
             chosen = jnp.where(source == part, found[part * width : (part + 1) * width], chosen)
-        value = value + chosen
-        for k in range(4):
-            value = value + cols[:, k : k + 1] * f_ref[k : k + 1, here]
-        hidden = swish_tanh(value)
+        hidden = swish_tanh(partial_sum[step] + chosen)
         ids = lax.broadcasted_iota(jnp.int32, (16, size), 0)
         side = jnp.where(upper, 1, 0)
         spread = jnp.concatenate(
@@ -345,7 +380,7 @@
             ],
             axis=0,
         )
-        acc[...] += dot_dims(spread, picks, 1, 1)
+        acc[...] += dot_dims(spread, recv_picks[step], 1, 1)
 
     def share_sums(layer):
         for owner in range(feats):
@@ -380,27 +415,29 @@
         return (latent.astype(F32) + normed).astype(BF)
 
     set_receivers(0, mesh_ref[...])
+    size = send_picks.shape[2]
+    steps = gs_ref.shape[1] // size
+    shift_first = slots.bit_length() - 1
+
+    @pl.loop(0, steps)
+    def begin(step):
+        pick_edges(step, gs_ref, gr_ref, shift_first)
+        start_edges(step, gr_ref, gf_ref)
+
     for copy in tile_copies:
         copy.wait()
-    size = 512
-    steps = gs_ref.shape[1] // size
-    shift_first = slots.bit_length() - 1
-
-    @pl.loop(0, steps // 2)
-    def first_half(step):
-        edge_block(step * size, size, gs_ref, gr_ref, gf_ref, tab[...].reshape(regions * width, slots), shift_first)
-
     for copy in first_hops[0][0]:
         copy.wait_recv()
     for copy in forwards[0]:
         copy.start()
 
-    @pl.loop(steps // 2, steps)
-    def second_half(step):
-        edge_block(step * size, size, gs_ref, gr_ref, gf_ref, tab[...].reshape(regions * width, slots), shift_first)
+    @pl.loop(0, steps)
+    def finish(step):
+        table = tab[...].reshape(regions * width, slots)
+        finish_edges(step, gs_ref, gr_ref, table, shift_first)
 
     sums = share_sums(0)
-    for copy in first_hops[0][1] + forwards[0] + sums + bias_copies:
+    for copy in keeps + first_hops[0][1] + forwards[0] + sums + bias_copies:
         copy.wait()
     for copy in first_hops[1][0]:
         copy.wait_recv()
@@ -413,6 +450,14 @@
     )
     for copy in enc_copies:
         copy.start()
+    mcap = tab2.shape[2]
+    shift_second = (2 * mcap).bit_length() - 1
+    mesh_steps = ms_ref.shape[1] // size
+
+    @pl.loop(0, mesh_steps)
+    def pick_mesh(step):
+        pick_edges(step, ms_ref, mr_ref, shift_second)
+
     for copy in id_copies + enc_copies:
         copy.wait()
     whole = enc[...].reshape(nodes, -1)
@@ -427,20 +472,23 @@
         copy.start()
     tab2[reg] = stage2[reg]
     set_receivers(1, whole)
+
+    @pl.loop(0, mesh_steps)
+    def begin_mesh(step):
+        start_edges(step, mr_ref, mf_ref)
+
     for owner in range(feats):
         out_enc[owner * rows : (owner + 1) * rows, :] = enc[owner, :, pl.ds(pl.multiple_of(ft * width, width), width)]
     for copy in row_copies:
         copy.wait()
-    mcap = tab2.shape[2]
     for part in range(regions):
         fold2[
             (part // 2) * width : (part // 2 + 1) * width, (part % 2) * mcap : (part % 2 + 1) * mcap
         ] = tab2[part]
-    shift_second = (2 * mcap).bit_length() - 1
-
-    @pl.loop(0, ms_ref.shape[1] // size)
-    def mesh_steps(step):
-        edge_block(step * size, size, ms_ref, mr_ref, mf_ref, fold2[...], shift_second)
+
+    @pl.loop(0, mesh_steps)
+    def finish_mesh(step):
+        finish_edges(step, ms_ref, mr_ref, fold2[...], shift_second)
 
     sums = share_sums(1)
     for copy in first_hops[1][1] + forwards[1] + sums:
@@ -472,7 +520,10 @@
     args = list(args)
     for at in (3, 4, 7, 8):
         args[at] = args[at].reshape(1, -1)
-    specs = [pl.BlockSpec(memory_space=pltpu.VMEM)] * len(args)
+    size = EDGE_BLOCK
+    steps = max(args[3].shape[1], args[7].shape[1]) // size
+    staged = [args[at] for at in (0, 10, 1, 11, 12, 13, 3, 4, 5, 6, 7, 8, 9, 15, 18, 20, 21, 22)]
+    specs = [pl.BlockSpec(memory_space=pltpu.HBM)] * len(args)
     specs[2] = pl.BlockSpec(memory_space=pltpu.SMEM)
     dma = pltpu.SemaphoreType.DMA
     vm = pltpu.VMEM
@@ -503,6 +554,11 @@
             vm((regions // 2 * width, 2 * mcap), BF),
             vm((feats, rows, width), BF),
             vm((feats, rows, width), BF),
+            vm((steps, slots, size), BF),
+            vm((steps, nodes // 2, size), BF),
+            vm((steps, width, size), F32),
+            *[vm(value.shape, value.dtype) for value in staged],
+            dma((len(staged),)), dma((2, 4)),
             dma((regions - 1,)), dma((regions - 1,)),
             dma((regions - 1,)), dma((regions - 1,)),
             dma((2, 3, 4)), dma((2, 3, 4)),
@@ -513,15 +569,16 @@
             dma((feats - 1,)), dma((feats - 1,)),
         ],
         compiler_params=pltpu.CompilerParams(
-            collective_id=0, has_side_effects=True, vmem_limit_bytes=48 << 20
+            collective_id=0, has_side_effects=True, vmem_limit_bytes=60 << 20
         ),
     )(*args)
 
 
 def pick_form(regions, feats, *args):
     width = args[10].shape[2]
+    even = args[3].shape[0] % EDGE_BLOCK == 0 and args[7].shape[0] % EDGE_BLOCK == 0
     rows = args[1].shape[0] // feats
-    if feats == 4 and width == 128 and rows == 128 and regions % 2 == 0 and regions <= 8:
+    if feats == 4 and width == 128 and rows == 128 and even and regions in (2, 4):
         return fused_device(regions, feats, *args)
     return per_device(*args)
 

time: 103 us -> 66.6 us (0.65)
  Pallas kernels: 80.5 us -> 62.7 us
  local copies, waits for them, and re-layouts: 20.8 us -> 3.14 us
    pallas_call x1, Pallas kernels: 80.5 us -> 62.7 us  [fused_device(): pl.pallas_call(functools.partial(fused, regions, feats), out_shape=(jax.S...]
    unnamed x48 -> x2, local copies, waits for them, and re-layouts: 20.8 us -> 3.14 us
where the time goes in v2:
time: 66.6 us; the launch traced here: 66.5 us
  Pallas kernels  62.7 us (94%)
  local copies, waits for them, and re-layouts  3.14 us (5%)
    pallas_call x1, Pallas kernels, fused_device(): pl.pallas_call(functools.partial(fused, regions, feats), out_shape=(jax.S...  62.7 us
    unnamed x2, local copies, waits for them, and re-layouts  3.14 us

profile of v2, /device:TPU:0, one launch (start us, length us, event | category | flops | bytes accessed | tf_op | source)
XLA Modules:
  0.0 66.5 jit_solution(6135455987372280115)
XLA Ops:
  0.6 62.7 %shard_map.230 = (bf16[512,128]{1,0:T(8,128)(2,1)}, bf16[512,128]{1,0:T(8,128)(2,1)}) custom-call(bf16[2048,512]{1,0:T(8,128)(2,1)} %grid_hbm.1, bf16[512,512]{1,0:T(8,128)(2,1)} %mesh_hbm.1, s32[1,4,4]{2,1,0:T(4,128)} %tiles_ref.1, s32[1,16384]{1,0:T(1,128)} %bitcast.4, s32[1,16384]{1,0:T(1,128)} %bitcast.5, f32[4,16384]{1,0:T(4,128)} %gf_hbm.1, ...), custom_call_target="tpu_custom_call" | custom-call | tf_op jit(solution)/shard_map/pallas_call | solution.py:530
  63.3 1.6 %copy.27 = bf16[512,128]{1,0:T(8,128)(2,1)} copy(bf16[512,128]{1,0:T(8,128)(2,1)} %get-tuple-element.4) | data formatting | bytes 262144
  64.9 1.6 %copy.28 = bf16[512,128]{1,0:T(8,128)(2,1)} copy(bf16[512,128]{1,0:T(8,128)(2,1)} %get-tuple-element.5) | data formatting | bytes 262144

commit v3 on v2

--- a/solution.py
+++ b/solution.py
@@ -181,7 +181,7 @@
 
 MESH = pl.DeviceIdType.MESH
 BF = jnp.bfloat16
-EDGE_BLOCK = 2048
+EDGE_BLOCK = 4096
 F32 = jnp.float32
 
 
@@ -297,7 +297,8 @@
 
     @pl.loop(0, grid_ref.shape[0] // 512)
     def project(step):
-        block = dot_dims(w_send[0], grid_ref[pl.ds(step * 512, 512), :], 0, 1).astype(BF)
+        rows_here = grid_ref[pl.ds(step * 512, 512), :]
+        block = jnp.dot(rows_here, w_send[0], preferred_element_type=F32).T.astype(BF)
         for part in range(512 // TILE):
             proj[step * (512 // TILE) + part] = block[:, part * TILE : (part + 1) * TILE]
 
@@ -369,13 +370,13 @@
         chosen = found[:width]
         for part in range(1, table.shape[0] // width):
             chosen = jnp.where(source == part, found[part * width : (part + 1) * width], chosen)
-        hidden = swish_tanh(partial_sum[step] + chosen)
+        hidden = swish_tanh(partial_sum[step] + chosen).astype(BF)
         ids = lax.broadcasted_iota(jnp.int32, (16, size), 0)
         side = jnp.where(upper, 1, 0)
         spread = jnp.concatenate(
             [
-                jnp.where(upper, 0.0, hidden).astype(BF),
-                jnp.where(upper, hidden, 0.0).astype(BF),
+                hidden * jnp.where(upper, 0.0, 1.0).astype(BF),
+                hidden * jnp.where(upper, 1.0, 0.0).astype(BF),
                 jnp.where(ids == side, 1.0, 0.0).astype(BF),
             ],
             axis=0,
@@ -445,10 +446,11 @@
         copy.start()
     mine = pl.ds(pl.multiple_of(ft * rows, rows), rows)
     enc[ft] = node_rows(0, mesh_ref[mine, :])
-    enc_copies = to_peers(
-        "feat", ft, feats, lambda p: enc.at[ft], lambda m: enc.at[m], e_ssem, e_rsem
-    )
-    for copy in enc_copies:
+    enc_copies = [
+        remote(enc.at[slot], enc.at[slot], e_ssem.at[at], e_rsem.at[at], "feat", peer)
+        for at, (slot, peer) in enumerate(((ft, across), (ft, partner), (across, partner)))
+    ]
+    for copy in enc_copies[:2]:
         copy.start()
     mcap = tab2.shape[2]
     shift_second = (2 * mcap).bit_length() - 1
@@ -458,7 +460,10 @@
     def pick_mesh(step):
         pick_edges(step, ms_ref, mr_ref, shift_second)
 
-    for copy in id_copies + enc_copies:
+    enc_copies[0].wait_recv()
+    enc_copies[2].start()
+    enc_copies[0].wait_send()
+    for copy in id_copies + enc_copies[1:]:
         copy.wait()
     whole = enc[...].reshape(nodes, -1)
     sent = dot_dims(w_send[1], whole, 0, 1).astype(BF)

time: 66.6 us -> 64.7 us (0.971)
  Pallas kernels: 62.7 us -> 60.8 us
    pallas_call x1, Pallas kernels: 62.7 us -> 60.8 us  [fused_device(): pl.pallas_call(functools.partial(fused, regions, feats), out_shape=(jax.S...]
where the time goes in v3:
time: 64.7 us; the launch traced here: 64.5 us
  Pallas kernels  60.8 us (94%)
  local copies, waits for them, and re-layouts  3.14 us (5%)
  between operations  0.65 us (1%)
    pallas_call x1, Pallas kernels, fused_device(): pl.pallas_call(functools.partial(fused, regions, feats), out_shape=(jax.S...  60.8 us
    unnamed x2, local copies, waits for them, and re-layouts  3.14 us

profile of v3, /device:TPU:0, one launch (start us, length us, event | category | flops | bytes accessed | tf_op | source)
XLA Modules:
  0.0 64.5 jit_solution(9321395228613567332)
XLA Ops:
  0.6 60.8 %shard_map.230 = (bf16[512,128]{1,0:T(8,128)(2,1)}, bf16[512,128]{1,0:T(8,128)(2,1)}) custom-call(bf16[2048,512]{1,0:T(8,128)(2,1)} %grid_hbm.1, bf16[512,512]{1,0:T(8,128)(2,1)} %mesh_hbm.1, s32[1,4,4]{2,1,0:T(4,128)} %tiles_ref.1, s32[1,16384]{1,0:T(1,128)} %bitcast.4, s32[1,16384]{1,0:T(1,128)} %bitcast.5, f32[4,16384]{1,0:T(4,128)} %gf_hbm.1, ...), custom_call_target="tpu_custom_call" | custom-call | tf_op jit(solution)/shard_map/pallas_call | solution.py:535
  61.4 1.6 %copy.27 = bf16[512,128]{1,0:T(8,128)(2,1)} copy(bf16[512,128]{1,0:T(8,128)(2,1)} %get-tuple-element.4) | data formatting | bytes 262144
  63.0 1.6 %copy.28 = bf16[512,128]{1,0:T(8,128)(2,1)} copy(bf16[512,128]{1,0:T(8,128)(2,1)} %get-tuple-element.5) | data formatting | bytes 262144
